TPU v7x, 256 devices: a whole 4x4x8 slice. The times are simulated.
256 devices in a mesh: bead: 32 (over z_hi, x, core), dom: 8 (over y, z_lo).
Axes of the slice: x: 4, y: 4, z: 8 (z_hi: 4, z_lo: 2; z = z_hi * 2 + z_lo), core: 2. Of those that a mesh axis runs over, the one named last changes fastest.
Arguments:
- positions: float32 [3, 32, 4096], P(None, 'bead', 'dom'), may hold values from -2.5 to 2.5
- momenta: float32 [3, 32, 4096], P(None, 'bead', 'dom'), may hold values from -6 to 6
- forces: float32 [3, 32, 4096], P(None, 'bead', 'dom'), may hold values from -6 to 6
- masses: float32 [4096], P('dom'), may hold values from 1 to 16
- charges: float32 [4096], P('dom'), may hold values from -1 to 1
- embedding: bfloat16 [4096, 240], P('dom'), may hold values from -6 to 6
- neighbours: int32 [8, 4096], P(None, 'dom'), may hold values from 0 to 895
- send_rows: int32 [3072], P('dom'), may hold values from 0 to 511
- wavevectors: int32 [3, 16384], replicated, may hold values from -12 to 12, as said below
- radial_weight: bfloat16 [2, 16, 240], replicated, may hold values from -1.5 to 1.5
- mix_weight: bfloat16 [2, 240, 240], replicated, may hold values from -0.375 to 0.375
- update_weight: bfloat16 [2, 240, 240], replicated, may hold values from -0.375 to 0.375
- readout_weight: bfloat16 [240, 240], replicated, may hold values from -0.375 to 0.375
- energy_weight: float32 [240], replicated, may hold values from -0.375 to 0.375
Outputs:
- next_positions: float32 [3, 32, 4096], P(None, 'bead', 'dom')
- next_momenta: float32 [3, 32, 4096], P(None, 'bead', 'dom')
- next_forces: float32 [3, 32, 4096], P(None, 'bead', 'dom')
Inputs may be any that keep to these rules, and one draw needn't show every extreme that they name: `wavevectors`: no component is zero.
All inputs are finite; a program needn't handle non-finite values.
Results may differ from a plain program's by a relative error of at most 0.0065.
Values may be sent and summed in bfloat16 or wider, within the bound.
A program may use at most 64 MiB of HBM per device.

v0:
```python
import math
import jax
import jax.numpy as jnp
from jax import lax
from jax.sharding import PartitionSpec as P

step_dt = 0.25
omega_cycle = 1.6
box_length = 4.0
ewald_sigma = 0.002
ewald_gain = 48.0
norm_eps = 1e-06
peak_frequency = lax.Precision.HIGHEST


def extended(cells, sides, width):
    for axis, dim in sides:
        count = lax.axis_size(axis)
        head = lax.slice_in_dim(cells, 0, width, axis=dim)
        tail = lax.slice_in_dim(cells, cells.shape[dim] - width, cells.shape[dim], axis=dim)
        cells = jnp.concatenate(
            [
                lax.ppermute(tail, axis, [(i, (i + 1) % count) for i in range(count)]),
                cells,
                lax.ppermute(head, axis, [((i + 1) % count, i) for i in range(count)]),
            ],
            axis=dim,
        )
    return cells


def mode_matrix(length):
    row_index = jnp.arange(length, dtype=jnp.int32)[:, None]
    column_index = jnp.arange(length, dtype=jnp.int32)[None, :]
    angles = 2.0 * math.pi / length * (row_index * column_index % length).astype(jnp.float32)
    single_norm = math.sqrt(1.0 / length)
    double_norm = math.sqrt(2.0 / length)
    parity = (1 - 2 * (row_index % 2)).astype(jnp.float32)
    middle = length // 2
    normal_transform = jnp.where(
        column_index == 0,
        single_norm,
        jnp.where(
            column_index < middle,
            double_norm * jnp.cos(angles),
            jnp.where(column_index == middle, single_norm * parity, double_norm * jnp.sin(angles)),
        ),
    )
    return normal_transform


def propagate(normal_mode_positions, normal_mode_momentum, masses):
    length = normal_mode_positions.shape[1]
    orders = jnp.arange(length, dtype=jnp.float32)
    omegas = 2.0 * omega_cycle * jnp.sin(math.pi * orders / length)
    cosine = jnp.cos(omegas * step_dt)[:, None]
    sines = jnp.sin(omegas * step_dt)
    omega_safe = jnp.where(orders == 0.0, 1.0, omegas)
    drift = jnp.where(orders == 0.0, step_dt, sines / omega_safe)[:, None]
    spring = (omegas * sines)[:, None]
    next_coords = cosine * normal_mode_positions + drift * normal_mode_momentum / masses
    next_moment = cosine * normal_mode_momentum - spring * masses * normal_mode_positions
    return (next_coords, next_moment)


def ewald_coef(reciprocal, atom_total):
    square = jnp.sum(reciprocal * reciprocal, 0)
    return (
        ewald_gain
        / math.sqrt(reciprocal.shape[1] * atom_total)
        * jnp.exp(-ewald_sigma * square)
        / square
    )


def phase_sums(reciprocal, centre, charge):
    phases = jnp.dot(reciprocal.T, centre, precision=peak_frequency)
    return (
        jnp.dot(jnp.cos(phases), charge, precision=peak_frequency),
        jnp.dot(jnp.sin(phases), charge, precision=peak_frequency),
    )


def ewald_force(reciprocal, centre, charge, cosine_sum, sine_sum, damping):
    phases = jnp.dot(reciprocal.T, centre, precision=peak_frequency)
    weight = (damping * cosine_sum)[:, None] * jnp.sin(phases) - (damping * sine_sum)[
        :, None
    ] * jnp.cos(phases)
    return 2.0 * charge * jnp.dot(reciprocal, weight, precision=peak_frequency)


def long_range(reciprocal, centre, charge, damping):
    cosine_part, sine_part = phase_sums(reciprocal, centre, charge)
    cosine_sum, sine_sum = lax.psum((cosine_part, sine_part), ("bead", "dom"))
    return ewald_force(reciprocal, centre, charge, cosine_sum, sine_sum, damping)


def advance(normal_mode_entries, mass_share, charge_share, reciprocal, damping):
    normal_mode_positions, normal_mode_momentum = propagate(
        normal_mode_entries[:3], normal_mode_entries[3:], mass_share
    )
    centre = normal_mode_positions[:, 0, :] / math.sqrt(normal_mode_entries.shape[1])
    long_force = long_range(reciprocal, centre, charge_share, damping)
    return (jnp.concatenate([normal_mode_positions, normal_mode_momentum], 0), long_force)


def layer_apply(
    hidden_own,
    extended_rows,
    extended_coords,
    neighbour_table,
    radial,
    mixing,
    update,
    radial_rates,
):
    owned_count = hidden_own.shape[0]
    owners = extended_coords[:, :owned_count]
    others = extended_coords[:, neighbour_table]
    offset = others - owners[:, None, :]
    distance = jnp.sum(offset * offset, 0)
    basis = (1.0 / (1.0 + radial_rates[:, None, None] * distance[None])).astype(jnp.bfloat16)
    edge_weight = jnp.einsum("mka,mf->kaf", basis, radial, preferred_element_type=jnp.float32)
    message = jnp.sum(edge_weight * extended_rows[neighbour_table], 0)
    scaled = message * lax.rsqrt(jnp.mean(message * message, -1, keepdims=True) + norm_eps)
    gated = jax.nn.silu(
        jnp.dot(scaled.astype(jnp.bfloat16), mixing, preferred_element_type=jnp.float32)
    ).astype(jnp.bfloat16)
    return hidden_own + jnp.dot(gated, update, preferred_element_type=jnp.float32)


def readout(hidden, readout_weight, energy_weight):
    activation = jax.nn.silu(
        jnp.dot(hidden.astype(jnp.bfloat16), readout_weight, preferred_element_type=jnp.float32)
    )
    return jnp.sum(activation * energy_weight)


def short_forces(
    coords,
    embedding,
    neighbours,
    send_rows,
    radial_weight,
    mix_weight,
    update_weight,
    readout_weight,
    energy_weight,
):
    owned_rows = coords.shape[2]
    ghost_rows = send_rows.shape[0] // 2
    to_before = send_rows[:ghost_rows]
    to_after = send_rows[ghost_rows:]
    radial_rates = 0.125 * 2.0 ** (0.5 * jnp.arange(radial_weight.shape[1], dtype=jnp.float32))
    apply_layer = jax.vmap(layer_apply, in_axes=(0, 0, 0, None, None, None, None, None))
    beside_all = extended(coords[:, :, send_rows], (("dom", 2),), ghost_rows)
    extended_coords = jnp.concatenate(
        [coords, beside_all[:, :, :ghost_rows], beside_all[:, :, 3 * ghost_rows :]], 2
    )
    extended_coords = jnp.moveaxis(extended_coords, 1, 0)
    hidden = embedding.astype(jnp.float32)[None]
    stored = []
    for number in range(mix_weight.shape[0]):
        rounded = hidden.astype(jnp.bfloat16)
        arrived = extended(rounded[:, send_rows, :], (("dom", 1),), ghost_rows)
        extended_rows = jnp.concatenate(
            [rounded, arrived[:, :ghost_rows], arrived[:, 3 * ghost_rows :]], 1
        ).astype(jnp.float32)
        stored.append((hidden, extended_rows))
        hidden = apply_layer(
            hidden,
            extended_rows,
            extended_coords,
            neighbours,
            radial_weight[number],
            mix_weight[number],
            update_weight[number],
            radial_rates,
        )
    cotan = jax.vmap(jax.grad(readout), in_axes=(0, None, None))(
        hidden, readout_weight, energy_weight
    )
    position_grad = jnp.zeros_like(extended_coords)
    for number in reversed(range(mix_weight.shape[0])):
        layer_input, extended_rows = stored[number]

        def local_layer(hidden_part, rows_part, coords_part):
            return apply_layer(
                hidden_part,
                rows_part,
                coords_part,
                neighbours,
                radial_weight[number],
                mix_weight[number],
                update_weight[number],
                radial_rates,
            )

        unused, pullback = jax.vjp(local_layer, layer_input, extended_rows, extended_coords)
        input_grad, feature_grad, position_part = pullback(cotan)
        position_grad = position_grad + position_part
        if number > 0:
            returned = extended(
                feature_grad[:, owned_rows:, :].astype(jnp.bfloat16), (("dom", 1),), ghost_rows
            ).astype(jnp.float32)
            owned_grad = (
                feature_grad[:, :owned_rows, :]
                .at[:, to_before, :]
                .add(returned[:, :ghost_rows])
                .at[:, to_after, :]
                .add(returned[:, 3 * ghost_rows :])
            )
            cotan = input_grad + owned_grad.astype(jnp.bfloat16).astype(jnp.float32)
    returned = extended(position_grad[:, :, owned_rows:], (("dom", 2),), ghost_rows)
    owned_force = (
        position_grad[:, :, :owned_rows]
        .at[:, :, to_before]
        .add(returned[:, :, :ghost_rows])
        .at[:, :, to_after]
        .add(returned[:, :, 3 * ghost_rows :])
    )
    return -jnp.moveaxis(owned_force, 0, 1)


def local(
    positions,
    momenta,
    forces,
    masses,
    charges,
    embedding,
    neighbours,
    send_rows,
    wavevectors,
    radial_weight,
    mix_weight,
    update_weight,
    readout_weight,
    energy_weight,
):
    beads_here = positions.shape[1]
    atom_count = positions.shape[2]
    bead_devices = lax.axis_size("bead")
    bead_slot = lax.axis_index("bead")
    bead_count = beads_here * bead_devices
    atom_share = atom_count // bead_devices
    normal_transform = mode_matrix(bead_count)
    bead_rows = lax.dynamic_slice_in_dim(normal_transform, bead_slot * beads_here, beads_here, 0)
    mass_share = lax.dynamic_slice_in_dim(masses, bead_slot * atom_share, atom_share, 0)
    charge_share = lax.dynamic_slice_in_dim(charges, bead_slot * atom_share, atom_share, 0)
    reciprocal = wavevectors.astype(jnp.float32) * (2.0 * math.pi / box_length)
    damping = ewald_coef(reciprocal, atom_count * lax.axis_size("dom"))
    coords_now, moment_now, force_now = (positions, momenta, forces)
    kicked = moment_now + 0.5 * step_dt * force_now
    stacked_arrays = jnp.concatenate([coords_now, kicked], 0)
    segment = stacked_arrays
    summed = lax.psum_scatter(
        jnp.einsum("bk,cba->ack", bead_rows, segment, precision=peak_frequency),
        "bead",
        scatter_dimension=0,
        tiled=True,
    )
    normal_mode_entries = jnp.transpose(summed, (1, 2, 0))
    joined, long_force = advance(normal_mode_entries, mass_share, charge_share, reciprocal, damping)
    packed = jnp.concatenate(
        [jnp.transpose(joined, (2, 0, 1)).reshape(atom_share, 6 * bead_count), long_force.T], 1
    )
    segment = lax.all_gather(packed, "bead", axis=0, tiled=True)
    row_count = segment.shape[0]
    coords = segment[:, : 6 * bead_count].reshape(row_count, 6, bead_count)
    restored = jnp.einsum("bk,ack->cba", bead_rows, coords, precision=peak_frequency)
    spread = segment[:, 6 * bead_count :].T[:, None, :]
    arrived = jnp.concatenate([restored, spread], 0)
    coords_now = arrived[:3]
    short_force = short_forces(
        coords_now,
        embedding,
        neighbours,
        send_rows,
        radial_weight,
        mix_weight,
        update_weight,
        readout_weight,
        energy_weight,
    )
    force_now = short_force + arrived[6:]
    moment_now = arrived[3:6] + 0.5 * step_dt * force_now
    return (coords_now, moment_now, force_now)


def solution(mesh):
    placed = (
        P(None, "bead", "dom"),
        P(None, "bead", "dom"),
        P(None, "bead", "dom"),
        P("dom"),
        P("dom"),
        P("dom", None),
        P(None, "dom"),
        P("dom"),
        P(),
        P(),
        P(),
        P(),
        P(),
        P(),
    )
    return jax.shard_map(
        local,
        mesh=mesh,
        in_specs=placed,
        out_specs=(P(None, "bead", "dom"), P(None, "bead", "dom"), P(None, "bead", "dom")),
        check_vma=False,
    )
```

profile of v0, /device:TPU:2, one launch (start us, length us, event | category | flops | bytes accessed | tf_op | source)
XLA Modules:
  0.0 636.9 jit_solution(1569555388232173794)
XLA Ops:
  14.6 4.4 collective-permute-start.3
  21.1 85.0 %reduce-scatter.2.cloned.1.call-done = f32[16,6,32]{2,1,0:T(8,128)} async-done(((f32[512,6,32]{2,1,0:T(8,128)}), f32[16,6,32]{2,1,0:T(8,128)}) %reduce-scatter.2.cloned.1.call-update) | async-done | bytes 12304 | tf_op jit(solution)/shard_map/reduce_scatter | solution.py:257
  107.1 8.0 %fusion.207 = (f32[16384,16]{0,1:T(8,128)S(1)}, f32[16384,16]{0,1:T(8,128)S(1)}) fusion(f32[3,16]{1,0:T(4,128)S(1)} %fusion.160, s32[3,16384]{1,0:T(4,128)S(1)} %copy-done.11), kind=kOutput, calls=%fused_computation.258 | convolution fusion | flops 9535488 | bytes 2293952 | tf_op jit(solution)/shard_map/dot_general | solution.py:77
  117.8 240.3 %all-reduce.5.cloned.1.call-done = (f32[16384]{0:T(1024)}, f32[16384]{0:T(1024)}) async-done(((f32[16384]{0:T(1024)}, f32[16384]{0:T(1024)}), (f32[16384]{0:T(1024)}, f32[16384]{0:T(1024)})) %all-reduce.5.cloned.1.call-update) | async-done | bytes 131088 | tf_op jit(solution)/shard_map/psum | solution.py:94
  360.6 41.0 %all_gather.3 = f32[512,195]{1,0:T(8,128)S(1)} all-gather(f32[16,195]{1,0:T(8,128)S(1)} %pad_maximum_fusion.5), channel_id=1, replica_groups=mesh['bead'=32,'dom'=8] {'bead'}, dimensions={0}, use_global_device_ids=true | all-gather | bytes 411840 | tf_op jit(solution)/shard_map/all_gather | solution.py:268
  406.1 16.1 %gather_fusion.3 = f32[4096,240]{1,0:T(8,128)} fusion(f32[896,240]{1,0:T(8,128)S(1)} %fusion.95, s32[4096]{0:T(1024)S(1)} %broadcast_clamp_fusion), kind=kCustom, calls=%fused_computation.3 | custom fusion | bytes 7880704 | tf_op jit(solution)/shard_map/vmap()/gather | solution.py:124
  422.2 5.3 copy.144
  427.5 5.3 copy.134
  433.6 10.8 %gather_fusion.1 = f32[4096,3]{1,0:T(8,128)S(1)} fusion(f32[3,896]{0,1:T(8,128)S(1)} %get-tuple-element.32, s32[4096]{0:T(1024)S(1)} %broadcast_clamp_fusion), kind=kCustom, calls=%fused_computation.1 | custom fusion | bytes 114688 | tf_op jit(solution)/shard_map/jvp(vmap())/gather | solution.py:119
  452.0 4.0 collective-permute-start.5
  459.8 3.4 collective-permute-done.4
  465.7 16.1 %gather_fusion.5 = f32[4096,240]{1,0:T(8,128)} fusion(f32[896,240]{1,0:T(8,128)S(1)} %copy.137, s32[4096]{0:T(1024)S(1)} %broadcast_clamp_fusion), kind=kCustom, calls=%fused_computation.5 | custom fusion | bytes 7880704 | tf_op jit(solution)/shard_map/vmap()/gather | solution.py:124
  481.7 5.3 copy.139
  487.0 4.4 multiply_reduce_fusion
  501.7 4.7 broadcast_multiply_fusion
  506.4 5.2 copy.154
  511.6 23.1 %scatter_custom_fusion.1 = f32[896,240]{1,0:T(8,128)S(1)} fusion(s32[4096]{0:T(1024)S(1)} %bitcast.302, f32[4096,240]{1,0:T(8,128)} %bitcast.291, f32[]{:T(128)} %constant.51.clone.1), kind=kCustom, calls=%fused_computation.103 | custom fusion | flops 983040 | bytes 860672 | tf_op jit(solution)/shard_map/transpose(jvp(vmap()))/scatter-add | solution.py:124
  538.4 5.3 copy.140
  543.7 3.1 fusion.59
  548.6 3.9 scatter_custom_fusion.2
  552.5 3.5 scatter_custom_fusion.3
  563.7 3.1 add_multiply_fusion
  571.7 22.8 %scatter_fusion = f32[3,896]{0,1:T(8,128)S(1)} fusion(f32[3,896]{0,1:T(8,128)S(1)} %pad_bitcast_fusion.1, s32[4096]{0:T(1024)S(1)} %bitcast.303, f32[4096,3]{1,0:T(8,128)} %bitcast.288), kind=kCustom, calls=%fused_computation.6 | custom fusion | flops 12288 | bytes 163840 | tf_op jit(solution)/shard_map/transpose(jvp(vmap()))/scatter-add | solution.py:119
  594.6 21.9 %scatter_fusion.1 = f32[3,896]{0,1:T(8,128)} fusion(f32[3,896]{0,1:T(8,128)} %pad_bitcast_fusion, s32[4096]{0:T(1024)S(1)} %bitcast.304, f32[4096,3]{1,0:T(8,128)S(1)} %bitcast.287), kind=kCustom, calls=%fused_computation.10 | custom fusion | flops 12288 | bytes 163840 | tf_op jit(solution)/shard_map/transpose(jvp(vmap()))/scatter-add | solution.py:119
  (174 shorter events, 76.0 us)
Async XLA Ops:
  7.2 485.4 %copy-start = (bf16[240,240]{1,0:T(8,128)(2,1)S(1)}, bf16[240,240]{1,0:T(8,128)(2,1)}, u32[]{:S(2)}) copy-start(bf16[240,240]{1,0:T(8,128)(2,1)} %param.26) | copy-start | bytes 345604
  7.2 12.7 %copy-start.21 = (s32[8,512]{1,0:T(8,128)S(1)}, s32[8,512]{1,0:T(8,128)}, u32[]{:S(2)}) copy-start(s32[8,512]{1,0:T(8,128)} %param.20) | copy-start | bytes 49156
  7.2 12.7 %copy-start.27 = (f32[512]{0:T(512)S(1)}, f32[512]{0:T(512)}, u32[]{:S(2)}) copy-start(f32[512]{0:T(512)} %param.18) | copy-start | bytes 6148
  7.2 13.6 %copy-start.11 = (s32[3,16384]{1,0:T(4,128)S(1)}, s32[3,16384]{1,0:T(4,128)}, u32[]{:S(2)}) copy-start(s32[3,16384]{1,0:T(4,128)} %param.22) | copy-start | bytes 589828
  7.2 98.8 %reduce-scatter.2.cloned.1.call-start = ((), (), s32[]{:S(2)}) async-start(), calls=%async_computation.1 | async-start | bytes 2162688 | tf_op jit(solution)/shard_map/reduce_scatter | solution.py:257
  12.3 345.8 %all-reduce.5.cloned.1.call-start = ((), (), s32[]{:S(2)}) async-start(), calls=%async_computation.2 | async-start | bytes 262144 | tf_op jit(solution)/shard_map/psum | solution.py:94
  14.6 391.4 %collective-permute-start.3 = (bf16[1,192,240]{2,1,0:T(8,128)(2,1)S(1)}, bf16[1,192,240]{2,1,0:T(8,128)(2,1)S(1)}, u32[]{:S(2)}, u32[]{:S(2)}) collective-permute-start(bf16[1,192,240]{2,1,0:T(8,128)(2,1)S(1)} %get-tuple-element.38), channel_id=1, source_target_pairs={{1,0},{2,1},{3,2},{4,3},{5,4},{6,5},{7,6},{0,7},{9,8},{10,9},{11,1... | collective-permute-start | bytes 276488 | tf_op jit(solution)/shard_map/ppermute | solution.py:25
  19.1 387.0 %collective-permute-start.2 = (bf16[1,192,240]{2,1,0:T(8,128)(2,1)S(1)}, bf16[1,192,240]{2,1,0:T(8,128)(2,1)S(1)}, u32[]{:S(2)}, u32[]{:S(2)}) collective-permute-start(bf16[1,192,240]{2,1,0:T(8,128)(2,1)S(1)} %get-tuple-element.37), channel_id=1, source_target_pairs={{0,1},{1,2},{2,3},{3,4},{4,5},{5,6},{6,7},{7,0},{8,9},{9,10},{10,1... | collective-permute-start | bytes 276488 | tf_op jit(solution)/shard_map/ppermute | solution.py:23
  19.3 425.8 %copy-start.22 = (f32[16]{0:T(128)}, f32[16]{0:T(128)S(1)}, u32[]{:S(2)}) copy-start(f32[16]{0:T(128)S(1)} %power_multiply_fusion) | copy-start | bytes 196
  403.5 30.0 %collective-permute-start.1 = (f32[3,1,192]{0,2,1:T(8,128)S(1)}, f32[3,1,192]{0,2,1:T(8,128)S(1)}, u32[]{:S(2)}, u32[]{:S(2)}) collective-permute-start(f32[3,1,192]{0,2,1:T(8,128)S(1)} %get-tuple-element.36), channel_id=1, source_target_pairs={{1,0},{2,1},{3,2},{4,3},{5,4},{6,5},{7,6},{0,7},{9,8},{10,9},{11,1... | collective-permute-start | bytes 6920 | tf_op jit(solution)/shard_map/ppermute | solution.py:25
  405.4 28.1 %collective-permute-start = (f32[3,1,192]{0,2,1:T(8,128)S(1)}, f32[3,1,192]{0,2,1:T(8,128)S(1)}, u32[]{:S(2)}, u32[]{:S(2)}) collective-permute-start(f32[3,1,192]{0,2,1:T(8,128)S(1)} %get-tuple-element.35), channel_id=1, source_target_pairs={{0,1},{1,2},{2,3},{3,4},{4,5},{5,6},{6,7},{7,0},{8,9},{9,10},{10,1... | collective-permute-start | bytes 6920 | tf_op jit(solution)/shard_map/ppermute | solution.py:23
  432.8 12.3 %copy-start.18 = (bf16[2,16,240]{2,1,0:T(8,128)(2,1)S(1)}, bf16[2,16,240]{2,1,0:T(8,128)(2,1)}, u32[]{:S(2)}) copy-start(bf16[2,16,240]{2,1,0:T(8,128)(2,1)} %param.23) | copy-start | bytes 46084
  448.1 10.8 %copy-start.19 = (f32[512]{0:T(512)}, f32[512]{0:T(512)S(1)}, u32[]{:S(2)}) copy-start(f32[512]{0:T(512)S(1)} %multiply_reduce_fusion.6) | copy-start | bytes 6148
  452.0 7.8 %collective-permute-start.5 = (bf16[1,192,240]{1,2,0:T(8,128)(2,1)S(1)}, bf16[1,192,240]{1,2,0:T(8,128)(2,1)S(1)}, u32[]{:S(2)}, u32[]{:S(2)}) collective-permute-start(bf16[1,192,240]{1,2,0:T(8,128)(2,1)S(1)} %get-tuple-element.40), channel_id=1, source_target_pairs={{1,0},{2,1},{3,2},{4,3},{5,4},{6,5},{7,6},{0,7},{9,8},{10,9},{11,1... | collective-permute-start | bytes 276488 | tf_op jit(solution)/shard_map/ppermute | solution.py:25
  456.1 7.1 %collective-permute-start.4 = (bf16[1,192,240]{1,2,0:T(8,128)(2,1)S(1)}, bf16[1,192,240]{1,2,0:T(8,128)(2,1)S(1)}, u32[]{:S(2)}, u32[]{:S(2)}) collective-permute-start(bf16[1,192,240]{1,2,0:T(8,128)(2,1)S(1)} %get-tuple-element.39), channel_id=1, source_target_pairs={{0,1},{1,2},{2,3},{3,4},{4,5},{5,6},{6,7},{7,0},{8,9},{9,10},{10,1... | collective-permute-start | bytes 276488 | tf_op jit(solution)/shard_map/ppermute | solution.py:23
  536.4 12.2 %collective-permute-start.7 = (bf16[1,192,240]{2,1,0:T(8,128)(2,1)}, bf16[1,192,240]{2,1,0:T(8,128)(2,1)S(1)}, u32[]{:S(2)}, u32[]{:S(2)}) collective-permute-start(bf16[1,192,240]{2,1,0:T(8,128)(2,1)} %get-tuple-element.30), channel_id=1, source_target_pairs={{1,0},{2,1},{3,2},{4,3},{5,4},{6,5},{7,6},{0,7},{9,8},{10,9},{11,1... | collective-permute-start | bytes 276488 | tf_op jit(solution)/shard_map/ppermute | solution.py:25
  537.5 11.1 %collective-permute-start.6 = (bf16[1,192,240]{2,1,0:T(8,128)(2,1)}, bf16[1,192,240]{2,1,0:T(8,128)(2,1)}, u32[]{:S(2)}, u32[]{:S(2)}) collective-permute-start(bf16[1,192,240]{2,1,0:T(8,128)(2,1)} %get-tuple-element.29), channel_id=1, source_target_pairs={{0,1},{1,2},{2,3},{3,4},{4,5},{5,6},{6,7},{7,0},{8,9},{9,10},{10,1... | collective-permute-start | bytes 276488 | tf_op jit(solution)/shard_map/ppermute | solution.py:23
  543.7 13.4 %copy-start.3 = (f32[512,240]{0,1:T(8,128)S(1)}, f32[512,240]{0,1:T(8,128)}, u32[]{:S(2)}) copy-start(f32[512,240]{0,1:T(8,128)} %copy-done.2) | copy-start | bytes 1474564
  546.8 12.9 %copy-start.20 = (f32[512]{0:T(512)S(1)}, f32[512]{0:T(512)}, u32[]{:S(2)}) copy-start(f32[512]{0:T(512)} %copy-done.19) | copy-start | bytes 6148
  548.6 12.2 %copy-start.25 = (f32[16]{0:T(128)S(1)}, f32[16]{0:T(128)}, u32[]{:S(2)}) copy-start(f32[16]{0:T(128)} %copy-done.22) | copy-start | bytes 196
  569.0 59.0 %copy-start.7 = (f32[512,195]{1,0:T(8,128)S(1)}, f32[512,195]{1,0:T(8,128)}, u32[]{:S(2)}) copy-start(f32[512,195]{1,0:T(8,128)} %copy-done.6) | copy-start | bytes 1198084
  569.0 59.0 %copy-start.10 = (f32[1,512,6]{2,1,0:T(8,128)S(1)}, f32[1,512,6]{2,1,0:T(8,128)}, u32[]{:S(2)}) copy-start(f32[1,512,6]{2,1,0:T(8,128)} %copy-done.9) | copy-start | bytes 36868
  617.6 6.8 %collective-permute-start.8 = (f32[1,3,192]{1,2,0:T(8,128)S(1)}, f32[1,3,192]{1,2,0:T(8,128)S(1)}, u32[]{:S(2)}, u32[]{:S(2)}) collective-permute-start(f32[1,3,192]{1,2,0:T(8,128)S(1)} %get-tuple-element.28), channel_id=1, source_target_pairs={{0,1},{1,2},{2,3},{3,4},{4,5},{5,6},{6,7},{7,0},{8,9},{9,10},{10,1... | collective-permute-start | bytes 6920 | tf_op jit(solution)/shard_map/ppermute | solution.py:23
  619.1 7.2 %collective-permute-start.9 = (f32[1,3,192]{1,2,0:T(8,128)S(1)}, f32[1,3,192]{1,2,0:T(8,128)S(1)}, u32[]{:S(2)}, u32[]{:S(2)}) collective-permute-start(f32[1,3,192]{1,2,0:T(8,128)S(1)} %get-tuple-element.27), channel_id=1, source_target_pairs={{1,0},{2,1},{3,2},{4,3},{5,4},{6,5},{7,6},{0,7},{9,8},{10,9},{11,1... | collective-permute-start | bytes 6920 | tf_op jit(solution)/shard_map/ppermute | solution.py:25
  (18 other events, 65.4 us)
Sparse Core Ops, SparseCore 0:
  12.4 93.5 reduce-scatter.1
  117.8 240.2 all-reduce.4
where the time goes:
time: 645 us; the launch traced here: 637 us
  waiting for transfers between devices  332 us (51%)
  other arithmetic  107 us (17%)
  local copies, waits for them, and re-layouts  88.1 us (14%)
  blocking collectives  41 us (6%)
  matrix products  35.9 us (6%)
  starting transfers between devices  17.5 us (3%)
  between operations  15 us (2%)
    psum x1, waiting for transfers between devices, long_range(): cosine_sum, sine_sum = lax.psum((cosine_part, sine_part), ('bead', 'dom'))  240 us
    reduce_scatter x1, waiting for transfers between devices, local(): lax.psum_scatter(jnp.einsum('bk,cba->ack', bead_rows, segment, precision=...  85 us
    gather x6, local copies, waits for them, and re-layouts, layer_apply(): message = jnp.sum(edge_weight * extended_rows[neighbour_table], 0)  53.4 us
    scatter-add x2, other arithmetic, layer_apply(): others = extended_coords[:, neighbour_table]  44.7 us
    all_gather x1, blocking collectives, local(): segment = lax.all_gather(packed, 'bead', axis=0, tiled=True)  41 us
    scatter-add x1, other arithmetic, layer_apply(): message = jnp.sum(edge_weight * extended_rows[neighbour_table], 0)  23.1 us
    ppermute x5, starting transfers between devices, extended(): lax.ppermute(head, axis, [((i + 1) % count, i) for i in range(count)])  14.3 us
  transfers between devices with their start and end apart: 12, of which 5 were waited for; matrix products, arithmetic and copies ran while one was open for 10% of the time, Pallas kernels for 0%

commit v1 on v0

--- a/solution.py
+++ b/solution.py
@@ -1,3 +1,4 @@
+import functools
 import math
 import jax
 import jax.numpy as jnp
@@ -11,6 +12,15 @@
 ewald_gain = 48.0
 norm_eps = 1e-06
 peak_frequency = lax.Precision.HIGHEST
+
+
+def fit_hubs_by_axis(field_in, chip_axis, bus_axis):
+    for t in (chip_axis, bus_axis):
+        field_in = lax.psum(field_in, axis_name=t)
+    return field_in
+
+
+try_all_the_stages_all = functools.partial(fit_hubs_by_axis, chip_axis="bead", bus_axis="dom")
 
 
 def extended(cells, sides, width):
@@ -91,7 +101,7 @@
 
 def long_range(reciprocal, centre, charge, damping):
     cosine_part, sine_part = phase_sums(reciprocal, centre, charge)
-    cosine_sum, sine_sum = lax.psum((cosine_part, sine_part), ("bead", "dom"))
+    cosine_sum, sine_sum = try_all_the_stages_all((cosine_part, sine_part))
     return ewald_force(reciprocal, centre, charge, cosine_sum, sine_sum, damping)
 
 

time: 645 us -> 749 us (1.16)
  waiting for transfers between devices: 332 us -> 433 us
    psum x1 -> x2, waiting for transfers between devices: 240 us -> 341 us  [fit_hubs_by_axis(): field_in = lax.psum(field_in, axis_name=t)]
  transfers between devices with their start and end apart: 12 -> 13, of which waited for: 5 -> 6; matrix products, arithmetic and copies ran while one was open for 10% -> 8% of each run, Pallas kernels for 0% -> 0%
where the time goes in v1:
time: 749 us; the launch traced here: 738 us
  waiting for transfers between devices  433 us (58%)
  other arithmetic  107 us (14%)
  local copies, waits for them, and re-layouts  88.4 us (12%)
  blocking collectives  40.9 us (5%)
  matrix products  36 us (5%)
  starting transfers between devices  17.9 us (2%)
  between operations  14.7 us (2%)
    psum x2, waiting for transfers between devices, fit_hubs_by_axis(): field_in = lax.psum(field_in, axis_name=t)  341 us
    reduce_scatter x1, waiting for transfers between devices, local(): lax.psum_scatter(jnp.einsum('bk,cba->ack', bead_rows, segment, precision=...  85.2 us
    gather x6, local copies, waits for them, and re-layouts, layer_apply(): message = jnp.sum(edge_weight * extended_rows[neighbour_table], 0)  53.6 us
    scatter-add x2, other arithmetic, layer_apply(): others = extended_coords[:, neighbour_table]  44.7 us
    all_gather x1, blocking collectives, local(): segment = lax.all_gather(packed, 'bead', axis=0, tiled=True)  40.9 us
    scatter-add x1, other arithmetic, layer_apply(): message = jnp.sum(edge_weight * extended_rows[neighbour_table], 0)  23.1 us
  transfers between devices with their start and end apart: 13, of which 6 were waited for; matrix products, arithmetic and copies ran while one was open for 8% of the time, Pallas kernels for 0%

profile of v1, /device:TPU:2, one launch (start us, length us, event | category | flops | bytes accessed | tf_op | source)
XLA Modules:
  0.0 737.9 jit_solution(12056500386306194404)
XLA Ops:
  14.6 4.4 collective-permute-start.3
  20.8 85.2 %reduce-scatter.2.cloned.1.call-done = f32[16,6,32]{2,1,0:T(8,128)} async-done(((f32[512,6,32]{2,1,0:T(8,128)}), f32[16,6,32]{2,1,0:T(8,128)}) %reduce-scatter.2.cloned.1.call-update) | async-done | bytes 12304 | tf_op jit(solution)/shard_map/reduce_scatter | solution.py:267
  107.0 8.0 %fusion.207 = (f32[16384,16]{0,1:T(8,128)S(1)}, f32[16384,16]{0,1:T(8,128)S(1)}) fusion(f32[3,16]{1,0:T(4,128)S(1)} %fusion.160, s32[3,16384]{1,0:T(4,128)S(1)} %copy-done.11), kind=kOutput, calls=%fused_computation.258 | convolution fusion | flops 9535488 | bytes 2293952 | tf_op jit(solution)/shard_map/dot_general | solution.py:87
  117.9 257.2 %all-reduce.7.cloned.1.call-done = (f32[16384]{0:T(1024)}, f32[16384]{0:T(1024)}) async-done(((f32[16384]{0:T(1024)}, f32[16384]{0:T(1024)}), (f32[16384]{0:T(1024)}, f32[16384]{0:T(1024)})) %all-reduce.7.cloned.1.call-update) | async-done | bytes 131088 | tf_op jit(solution)/shard_map/psum | solution.py:19
  375.2 83.5 %all-reduce.9.cloned.1.call-done = (f32[16384]{0:T(1024)}, f32[16384]{0:T(1024)}) async-done(((f32[16384]{0:T(1024)}, f32[16384]{0:T(1024)}), (f32[16384]{0:T(1024)}, f32[16384]{0:T(1024)})) %all-reduce.9.cloned.1.call-update) | async-done | bytes 131088 | tf_op jit(solution)/shard_map/psum | solution.py:19
  461.2 40.9 %all_gather.3 = f32[512,195]{1,0:T(8,128)S(1)} all-gather(f32[16,195]{1,0:T(8,128)S(1)} %pad_maximum_fusion.5), channel_id=1, replica_groups=mesh['bead'=32,'dom'=8] {'bead'}, dimensions={0}, use_global_device_ids=true | all-gather | bytes 411840 | tf_op jit(solution)/shard_map/all_gather | solution.py:278
  506.9 16.2 %gather_fusion.3 = f32[4096,240]{1,0:T(8,128)} fusion(f32[896,240]{1,0:T(8,128)S(1)} %fusion.95, s32[4096]{0:T(1024)S(1)} %broadcast_clamp_fusion), kind=kCustom, calls=%fused_computation.3 | custom fusion | bytes 7880704 | tf_op jit(solution)/shard_map/vmap()/gather | solution.py:134
  523.0 5.3 copy.144
  528.3 5.3 copy.134
  534.4 10.8 %gather_fusion.1 = f32[4096,3]{1,0:T(8,128)S(1)} fusion(f32[3,896]{0,1:T(8,128)S(1)} %get-tuple-element.34, s32[4096]{0:T(1024)S(1)} %broadcast_clamp_fusion), kind=kCustom, calls=%fused_computation.1 | custom fusion | bytes 114688 | tf_op jit(solution)/shard_map/jvp(vmap())/gather | solution.py:129
  552.8 4.2 collective-permute-start.5
  560.8 3.4 collective-permute-done.4
  566.6 16.2 %gather_fusion.5 = f32[4096,240]{1,0:T(8,128)} fusion(f32[896,240]{1,0:T(8,128)S(1)} %copy.137, s32[4096]{0:T(1024)S(1)} %broadcast_clamp_fusion), kind=kCustom, calls=%fused_computation.5 | custom fusion | bytes 7880704 | tf_op jit(solution)/shard_map/vmap()/gather | solution.py:134
  582.8 5.3 copy.139
  588.1 4.4 multiply_reduce_fusion
  602.8 4.7 broadcast_multiply_fusion
  607.5 5.2 copy.154
  612.8 23.1 %scatter_custom_fusion.1 = f32[896,240]{1,0:T(8,128)S(1)} fusion(s32[4096]{0:T(1024)S(1)} %bitcast.302, f32[4096,240]{1,0:T(8,128)} %bitcast.291, f32[]{:T(128)} %constant.51.clone.1), kind=kCustom, calls=%fused_computation.103 | custom fusion | flops 983040 | bytes 860672 | tf_op jit(solution)/shard_map/transpose(jvp(vmap()))/scatter-add | solution.py:134
  639.5 5.3 copy.140
  649.8 3.9 scatter_custom_fusion.2
  653.7 3.5 scatter_custom_fusion.3
  664.9 3.2 add_multiply_fusion
  673.0 22.8 %scatter_fusion = f32[3,896]{0,1:T(8,128)S(1)} fusion(f32[3,896]{0,1:T(8,128)S(1)} %pad_bitcast_fusion.1, s32[4096]{0:T(1024)S(1)} %bitcast.303, f32[4096,3]{1,0:T(8,128)} %bitcast.288), kind=kCustom, calls=%fused_computation.6 | custom fusion | flops 12288 | bytes 163840 | tf_op jit(solution)/shard_map/transpose(jvp(vmap()))/scatter-add | solution.py:129
  695.8 21.9 %scatter_fusion.1 = f32[3,896]{0,1:T(8,128)} fusion(f32[3,896]{0,1:T(8,128)} %pad_bitcast_fusion, s32[4096]{0:T(1024)S(1)} %bitcast.304, f32[4096,3]{1,0:T(8,128)S(1)} %bitcast.287), kind=kCustom, calls=%fused_computation.10 | custom fusion | flops 12288 | bytes 163840 | tf_op jit(solution)/shard_map/transpose(jvp(vmap()))/scatter-add | solution.py:129
  (175 shorter events, 79.4 us)
Async XLA Ops:
  7.2 586.5 %copy-start = (bf16[240,240]{1,0:T(8,128)(2,1)S(1)}, bf16[240,240]{1,0:T(8,128)(2,1)}, u32[]{:S(2)}) copy-start(bf16[240,240]{1,0:T(8,128)(2,1)} %param.26) | copy-start | bytes 345604
  7.2 12.6 %copy-start.21 = (s32[8,512]{1,0:T(8,128)S(1)}, s32[8,512]{1,0:T(8,128)}, u32[]{:S(2)}) copy-start(s32[8,512]{1,0:T(8,128)} %param.20) | copy-start | bytes 49156
  7.2 12.6 %copy-start.26 = (f32[512]{0:T(512)S(1)}, f32[512]{0:T(512)}, u32[]{:S(2)}) copy-start(f32[512]{0:T(512)} %param.18) | copy-start | bytes 6148
  7.2 98.8 %reduce-scatter.2.cloned.1.call-start = ((), (), s32[]{:S(2)}) async-start(), calls=%async_computation.1 | async-start | bytes 2162688 | tf_op jit(solution)/shard_map/reduce_scatter | solution.py:267
  7.3 99.7 %copy-start.11 = (s32[3,16384]{1,0:T(4,128)S(1)}, s32[3,16384]{1,0:T(4,128)}, u32[]{:S(2)}) copy-start(s32[3,16384]{1,0:T(4,128)} %param.22) | copy-start | bytes 589828
  12.3 362.8 %all-reduce.7.cloned.1.call-start = ((), (), s32[]{:S(2)}) async-start(), calls=%async_computation.2 | async-start | bytes 262144 | tf_op jit(solution)/shard_map/psum | solution.py:19
  14.6 492.2 %collective-permute-start.3 = (bf16[1,192,240]{2,1,0:T(8,128)(2,1)S(1)}, bf16[1,192,240]{2,1,0:T(8,128)(2,1)S(1)}, u32[]{:S(2)}, u32[]{:S(2)}) collective-permute-start(bf16[1,192,240]{2,1,0:T(8,128)(2,1)S(1)} %get-tuple-element.40), channel_id=1, source_target_pairs={{1,0},{2,1},{3,2},{4,3},{5,4},{6,5},{7,6},{0,7},{9,8},{10,9},{11,1... | collective-permute-start | bytes 276488 | tf_op jit(solution)/shard_map/ppermute | solution.py:35
  19.0 487.7 %collective-permute-start.2 = (bf16[1,192,240]{2,1,0:T(8,128)(2,1)S(1)}, bf16[1,192,240]{2,1,0:T(8,128)(2,1)S(1)}, u32[]{:S(2)}, u32[]{:S(2)}) collective-permute-start(bf16[1,192,240]{2,1,0:T(8,128)(2,1)S(1)} %get-tuple-element.39), channel_id=1, source_target_pairs={{0,1},{1,2},{2,3},{3,4},{4,5},{5,6},{6,7},{7,0},{8,9},{9,10},{10,1... | collective-permute-start | bytes 276488 | tf_op jit(solution)/shard_map/ppermute | solution.py:33
  117.6 341.1 %all-reduce.9.cloned.1.call-start = ((), (), s32[]{:S(2)}) async-start(), calls=%async_computation.3 | async-start | bytes 262144 | tf_op jit(solution)/shard_map/psum | solution.py:19
  375.1 182.1 %copy-start.22 = (f32[16]{0:T(128)}, f32[16]{0:T(128)S(1)}, u32[]{:S(2)}) copy-start(f32[16]{0:T(128)S(1)} %power_multiply_fusion) | copy-start | bytes 196
  504.0 30.4 %collective-permute-start.1 = (f32[3,1,192]{0,2,1:T(8,128)S(1)}, f32[3,1,192]{0,2,1:T(8,128)S(1)}, u32[]{:S(2)}, u32[]{:S(2)}) collective-permute-start(f32[3,1,192]{0,2,1:T(8,128)S(1)} %get-tuple-element.38), channel_id=1, source_target_pairs={{1,0},{2,1},{3,2},{4,3},{5,4},{6,5},{7,6},{0,7},{9,8},{10,9},{11,1... | collective-permute-start | bytes 6920 | tf_op jit(solution)/shard_map/ppermute | solution.py:35
  506.3 28.1 %collective-permute-start = (f32[3,1,192]{0,2,1:T(8,128)S(1)}, f32[3,1,192]{0,2,1:T(8,128)S(1)}, u32[]{:S(2)}, u32[]{:S(2)}) collective-permute-start(f32[3,1,192]{0,2,1:T(8,128)S(1)} %get-tuple-element.37), channel_id=1, source_target_pairs={{0,1},{1,2},{2,3},{3,4},{4,5},{5,6},{6,7},{7,0},{8,9},{9,10},{10,1... | collective-permute-start | bytes 6920 | tf_op jit(solution)/shard_map/ppermute | solution.py:33
  533.6 12.3 %copy-start.18 = (bf16[2,16,240]{2,1,0:T(8,128)(2,1)S(1)}, bf16[2,16,240]{2,1,0:T(8,128)(2,1)}, u32[]{:S(2)}) copy-start(bf16[2,16,240]{2,1,0:T(8,128)(2,1)} %param.23) | copy-start | bytes 46084
  552.8 7.9 %collective-permute-start.5 = (bf16[1,192,240]{1,2,0:T(8,128)(2,1)S(1)}, bf16[1,192,240]{1,2,0:T(8,128)(2,1)S(1)}, u32[]{:S(2)}, u32[]{:S(2)}) collective-permute-start(bf16[1,192,240]{1,2,0:T(8,128)(2,1)S(1)} %get-tuple-element.42), channel_id=1, source_target_pairs={{1,0},{2,1},{3,2},{4,3},{5,4},{6,5},{7,6},{0,7},{9,8},{10,9},{11,1... | collective-permute-start | bytes 276488 | tf_op jit(solution)/shard_map/ppermute | solution.py:35
  557.0 7.1 collective-permute-start.4
  637.5 12.2 %collective-permute-start.7 = (bf16[1,192,240]{2,1,0:T(8,128)(2,1)}, bf16[1,192,240]{2,1,0:T(8,128)(2,1)S(1)}, u32[]{:S(2)}, u32[]{:S(2)}) collective-permute-start(bf16[1,192,240]{2,1,0:T(8,128)(2,1)} %get-tuple-element.32), channel_id=1, source_target_pairs={{1,0},{2,1},{3,2},{4,3},{5,4},{6,5},{7,6},{0,7},{9,8},{10,9},{11,1... | collective-permute-start | bytes 276488 | tf_op jit(solution)/shard_map/ppermute | solution.py:35
  638.7 11.1 %collective-permute-start.6 = (bf16[1,192,240]{2,1,0:T(8,128)(2,1)}, bf16[1,192,240]{2,1,0:T(8,128)(2,1)}, u32[]{:S(2)}, u32[]{:S(2)}) collective-permute-start(bf16[1,192,240]{2,1,0:T(8,128)(2,1)} %get-tuple-element.31), channel_id=1, source_target_pairs={{0,1},{1,2},{2,3},{3,4},{4,5},{5,6},{6,7},{7,0},{8,9},{9,10},{10,1... | collective-permute-start | bytes 276488 | tf_op jit(solution)/shard_map/ppermute | solution.py:33
  644.9 13.4 %copy-start.3 = (f32[512,240]{0,1:T(8,128)S(1)}, f32[512,240]{0,1:T(8,128)}, u32[]{:S(2)}) copy-start(f32[512,240]{0,1:T(8,128)} %copy-done.2) | copy-start | bytes 1474564
  648.0 12.9 %copy-start.20 = (f32[512]{0:T(512)S(1)}, f32[512]{0:T(512)}, u32[]{:S(2)}) copy-start(f32[512]{0:T(512)} %copy-done.19) | copy-start | bytes 6148
  649.8 12.3 %copy-start.24 = (f32[16]{0:T(128)S(1)}, f32[16]{0:T(128)}, u32[]{:S(2)}) copy-start(f32[16]{0:T(128)} %copy-done.22) | copy-start | bytes 196
  670.3 59.0 %copy-start.7 = (f32[512,195]{1,0:T(8,128)S(1)}, f32[512,195]{1,0:T(8,128)}, u32[]{:S(2)}) copy-start(f32[512,195]{1,0:T(8,128)} %copy-done.6) | copy-start | bytes 1198084
  670.3 59.1 %copy-start.10 = (f32[1,512,6]{2,1,0:T(8,128)S(1)}, f32[1,512,6]{2,1,0:T(8,128)}, u32[]{:S(2)}) copy-start(f32[1,512,6]{2,1,0:T(8,128)} %copy-done.9) | copy-start | bytes 36868
  718.8 6.8 collective-permute-start.8
  720.3 7.2 collective-permute-start.9
  (18 other events, 68.4 us)
Sparse Core Ops, SparseCore 0:
  12.4 93.5 reduce-scatter.1
  117.8 257.2 all-reduce.6
  377.9 80.7 all-reduce.8
